TPU v7x, 32 devices: a whole 2x2x4 slice. The times are simulated.
32 devices in a mesh: dp: 8 (over z, x), tensor: 4 (over y, core).
Axes of the slice: x: 2, y: 2, z: 4, core: 2. Of those that a mesh axis runs over, the one named last changes fastest.
Arguments:
- gate_grads: bfloat16 [8, 256, 8192], P('dp', 'tensor'), may hold values from -6 to 6
- up_grads: bfloat16 [8, 256, 8192], P('dp', 'tensor'), may hold values from -6 to 6
- gate_errors: bfloat16 [8, 256, 8192], P('dp', 'tensor'), may hold values from -3 to 3
- up_errors: bfloat16 [8, 256, 8192], P('dp', 'tensor'), may hold values from -3 to 3
- gate_start: float32 [8192, 32], replicated, may hold values from -6 to 6
- up_start: float32 [8192, 32], replicated, may hold values from -6 to 6
Outputs:
- gate_mean: bfloat16 [256, 8192], P('tensor')
- up_mean: bfloat16 [256, 8192], P('tensor')
- gate_new_errors: bfloat16 [8, 256, 8192], P('dp', 'tensor')
- up_new_errors: bfloat16 [8, 256, 8192], P('dp', 'tensor')
All inputs are finite; a program needn't handle non-finite values.
Results may differ from a plain program's by a relative error of at most 0.0015.
Values sent between devices are 32-bit elements; how exact they have to be, the bound alone decides.
A program may use at most 64 MiB of HBM per device.

v0:
```python
import jax
import jax.numpy as jnp
from jax import lax
from jax.sharding import PartitionSpec as P


def orthonormal(left, gram):
    lower = jnp.linalg.cholesky(gram)
    return lax.linalg.triangular_solve(lower, left, left_side=False, lower=True, transpose_a=True)


def inner(first, second):
    return jnp.dot(first.T, second, precision=lax.Precision.HIGHEST)


def per_device(gate_grads, up_grads, gate_errors, up_errors, gate_start, up_start):
    replicas = lax.axis_size("dp")
    gate_full = gate_grads[0].astype(jnp.float32) + gate_errors[0].astype(jnp.float32)
    up_full = up_grads[0].astype(jnp.float32) + up_errors[0].astype(jnp.float32)
    gate_term = jnp.dot(gate_full, gate_start, precision=lax.Precision.HIGHEST)
    up_term = jnp.dot(up_full, up_start, precision=lax.Precision.HIGHEST)
    gate_left, up_left = lax.psum((gate_term, up_term), "dp")
    gate_left = gate_left / replicas
    up_left = up_left / replicas
    gate_gram, up_gram = lax.psum((inner(gate_left, gate_left), inner(up_left, up_left)), "tensor")
    gate_basis = orthonormal(gate_left, gate_gram)
    up_basis = orthonormal(up_left, up_gram)
    gate_right, up_right = lax.psum(
        (inner(gate_full, gate_basis), inner(up_full, up_basis)), ("dp", "tensor")
    )
    gate_right = gate_right / replicas
    up_right = up_right / replicas
    gate_approx = jnp.dot(gate_basis, gate_right.T, precision=lax.Precision.HIGHEST)
    up_approx = jnp.dot(up_basis, up_right.T, precision=lax.Precision.HIGHEST)
    gate_new = (gate_full - gate_approx).astype(jnp.bfloat16)[None]
    up_new = (up_full - up_approx).astype(jnp.bfloat16)[None]
    return (gate_approx.astype(jnp.bfloat16), up_approx.astype(jnp.bfloat16), gate_new, up_new)


def solution(mesh):
    in_specs = (
        P("dp", "tensor", None),
        P("dp", "tensor", None),
        P("dp", "tensor", None),
        P("dp", "tensor", None),
        P(),
        P(),
    )
    out_specs = (
        P("tensor", None),
        P("tensor", None),
        P("dp", "tensor", None),
        P("dp", "tensor", None),
    )
    return jax.shard_map(
        per_device, mesh=mesh, in_specs=in_specs, out_specs=out_specs, check_vma=False
    )
```

profile of v0, /device:TPU:1, one launch (start us, length us, event | category | flops | bytes accessed | tf_op | source)
XLA Modules:
  0.0 227.5 jit_solution(3288730595172913577)
XLA Ops:
  7.2 1.2 copy-done
  8.4 3.6 %fusion.7 = f32[64,32]{0,1:T(8,128)S(1)} fusion(f32[8192,32]{0,1:T(8,128)S(1)} %copy-done, bf16[1,64,8192]{2,1,0:T(8,128)(2,1)} %param.11, bf16[1,64,8192]{2,1,0:T(8,128)(2,1)} %param.9), kind=kOutput, calls=%fused_computation.9 | convolution fusion | flops 202899456 | bytes 3153920 | tf_op jit(solution)/shard_map/dot_general | solution.py:20
  12.0 1.9 fusion.2
  14.0 31.1 %all-reduce.1 = (f32[64,32]{0,1:T(8,128)S(1)}, f32[64,32]{0,1:T(8,128)S(1)}) all-reduce(f32[64,32]{0,1:T(8,128)S(1)} %fusion.7, f32[64,32]{0,1:T(8,128)S(1)} %fusion.2), channel_id=1, replica_groups=mesh['dp'=8,'tensor'=4] {'dp'}, use_global_device_ids=true, to_apply=%region_0.0 | all-reduce | flops 4096 | bytes 32768 | tf_op jit(solution)/shard_map/psum | solution.py:22
  45.0 0.1 fusion.28
  45.2 0.1 fusion.25
  45.3 17.9 %all-reduce.2 = (f32[32,32]{0,1:T(8,128)S(1)}, f32[32,32]{0,1:T(8,128)S(1)}) all-reduce(f32[32,32]{0,1:T(8,128)S(1)} %fusion.28, f32[32,32]{0,1:T(8,128)S(1)} %fusion.25), channel_id=1, replica_groups=mesh['dp'=8,'tensor'=4] {'tensor'}, use_global_device_ids=true, to_apply=%region_1.0 | all-reduce | flops 2048 | bytes 16384 | tf_op jit(solution)/shard_map/psum | solution.py:25
  63.2 0.1 copy.15
  63.3 0.1 copy.17
  63.4 2.9 %cholesky.55 = f32[32,32]{1,0:T(8,128)S(1)} custom-call(f32[32,32]{1,0:T(8,128)S(1)} %get-tuple-element.16), custom_call_target="Cholesky" | custom-call | tf_op jit(solution)/shard_map/jit(cholesky)/cholesky | solution.py:8
  66.3 0.6 compare_reduce_fusion
  67.0 0.7 fusion.19
  67.6 2.4 %custom-call.7 = f32[1,32,32]{1,2,0:T(8,128)S(1)} custom-call(f32[1,32,32]{2,1,0:T(8,128)S(1)} %fusion.19), custom_call_target="InvertDiagBlocksLowerTriangular" | custom-call | tf_op jit(solution)/shard_map/triangular_solve/custom-call.0 | solution.py:9
  70.1 0.2 convolution_bitcast_fusion
  70.3 2.9 %cholesky.44 = f32[32,32]{1,0:T(8,128)S(1)} custom-call(f32[32,32]{1,0:T(8,128)S(1)} %get-tuple-element.17), custom_call_target="Cholesky" | custom-call | tf_op jit(solution)/shard_map/jit(cholesky)/cholesky | solution.py:8
  73.3 0.6 compare_reduce_fusion.1
  73.9 0.7 fusion.18
  74.6 2.4 %custom-call.6 = f32[1,32,32]{1,2,0:T(8,128)S(1)} custom-call(f32[1,32,32]{2,1,0:T(8,128)S(1)} %fusion.18), custom_call_target="InvertDiagBlocksLowerTriangular" | custom-call | tf_op jit(solution)/shard_map/triangular_solve/custom-call.0 | solution.py:9
  77.0 0.2 convolution_bitcast_fusion.1
  77.3 2.5 %fusion.5 = f32[8192,32]{0,1:T(8,128)} fusion(f32[64,32]{0,1:T(8,128)S(1)} %convolution_bitcast_fusion.1, bf16[1,64,8192]{2,1,0:T(8,128)(2,1)S(1)} %copy-done.1, bf16[1,64,8192]{2,1,0:T(8,128)(2,1)S(1)} %copy-done.2), kind=kOutput, calls=%fused_computation.7 | convolution fusion | flops 202899456 | bytes 3153920 | tf_op jit(solution)/shard_map/dot_general | solution.py:13
  79.8 2.5 %fusion = f32[8192,32]{0,1:T(8,128)} fusion(f32[64,32]{0,1:T(8,128)S(1)} %convolution_bitcast_fusion, bf16[1,64,8192]{2,1,0:T(8,128)(2,1)S(1)} %copy-done.4, bf16[1,64,8192]{2,1,0:T(8,128)(2,1)S(1)} %copy-done.7), kind=kOutput, calls=%fused_computation.1 | convolution fusion | flops 202899456 | bytes 3153920 | tf_op jit(solution)/shard_map/dot_general | solution.py:13
  82.3 130.3 %all-reduce.5.cloned.1.call-done = (f32[8192,32]{0,1:T(8,128)}, f32[8192,32]{0,1:T(8,128)}) async-done(((f32[8192,32]{0,1:T(8,128)}, f32[8192,32]{0,1:T(8,128)}), (f32[8192,32]{0,1:T(8,128)}, f32[8192,32]{0,1:T(8,128)})) %all-reduce.5.cloned.1.call-update) | async-done | bytes 2097168 | tf_op jit(solution)/shard_map/psum | solution.py:28
  212.6 4.7 %fusion.10 = (bf16[1,64,8192]{2,1,0:T(8,128)(2,1)}, bf16[64,8192]{1,0:T(8,128)(2,1)}) fusion(bf16[1,64,8192]{2,1,0:T(8,128)(2,1)S(1)} %copy-done.1, bf16[1,64,8192]{2,1,0:T(8,128)(2,1)S(1)} %copy-done.2, f32[64,32]{0,1:T(8,128)S(1)} %convolution_bitcast_fusion.1, f32[8192,32]{0,1:T(8,128)} %get-tuple-element.6), kind=kOutput, calls=%fused_computation.16 | convolution fusion | flops 204734464 | bytes 5251072 | tf_op jit(solution)/shard_map/dot_general | solution.py:33
  217.3 3.3 %fusion.11 = (bf16[1,64,8192]{2,1,0:T(8,128)(2,1)}, bf16[64,8192]{1,0:T(8,128)(2,1)}) fusion(bf16[1,64,8192]{2,1,0:T(8,128)(2,1)S(1)} %copy-done.5, bf16[1,64,8192]{2,1,0:T(8,128)(2,1)S(1)} %copy-done.8, f32[64,32]{0,1:T(8,128)S(1)} %convolution_bitcast_fusion, f32[8192,32]{0,1:T(8,128)S(1)} %copy-done.10), kind=kOutput, calls=%fused_computation.17 | convolution fusion | flops 204734464 | bytes 5251072 | tf_op jit(solution)/shard_map/dot_general | solution.py:34
  (26 shorter events, 0.2 us)
Async XLA Ops:
  7.2 1.2 copy-start
  7.2 205.4 %all-reduce.5.cloned.1.call-start = ((), (), s32[]{:S(2)}) async-start(), calls=%async_computation | async-start | bytes 4194304 | tf_op jit(solution)/shard_map/psum | solution.py:28
  8.4 3.6 %copy-start.3 = (bf16[1,64,8192]{2,1,0:T(8,128)(2,1)S(1)}, bf16[1,64,8192]{2,1,0:T(8,128)(2,1)}, u32[]{:S(2)}) copy-start(bf16[1,64,8192]{2,1,0:T(8,128)(2,1)} %param.12) | copy-start | bytes 3145732
  8.4 3.6 %copy-start.6 = (bf16[1,64,8192]{2,1,0:T(8,128)(2,1)S(1)}, bf16[1,64,8192]{2,1,0:T(8,128)(2,1)}, u32[]{:S(2)}) copy-start(bf16[1,64,8192]{2,1,0:T(8,128)(2,1)} %param.10) | copy-start | bytes 3145732
  8.4 3.6 %copy-start.9 = (f32[8192,32]{0,1:T(8,128)S(1)}, f32[8192,32]{0,1:T(8,128)}, u32[]{:S(2)}) copy-start(f32[8192,32]{0,1:T(8,128)} %param.14) | copy-start | bytes 3145732
  12.0 65.2 %copy-start.1 = (bf16[1,64,8192]{2,1,0:T(8,128)(2,1)S(1)}, bf16[1,64,8192]{2,1,0:T(8,128)(2,1)}, u32[]{:S(2)}) copy-start(bf16[1,64,8192]{2,1,0:T(8,128)(2,1)} %param.11) | copy-start | bytes 3145732
  12.0 65.2 %copy-start.2 = (bf16[1,64,8192]{2,1,0:T(8,128)(2,1)S(1)}, bf16[1,64,8192]{2,1,0:T(8,128)(2,1)}, u32[]{:S(2)}) copy-start(bf16[1,64,8192]{2,1,0:T(8,128)(2,1)} %param.9) | copy-start | bytes 3145732
  77.3 2.5 %copy-start.4 = (bf16[1,64,8192]{2,1,0:T(8,128)(2,1)S(1)}, bf16[1,64,8192]{2,1,0:T(8,128)(2,1)}, u32[]{:S(2)}) copy-start(bf16[1,64,8192]{2,1,0:T(8,128)(2,1)} %param.12) | copy-start | bytes 3145732
  77.3 2.5 %copy-start.7 = (bf16[1,64,8192]{2,1,0:T(8,128)(2,1)S(1)}, bf16[1,64,8192]{2,1,0:T(8,128)(2,1)}, u32[]{:S(2)}) copy-start(bf16[1,64,8192]{2,1,0:T(8,128)(2,1)} %param.10) | copy-start | bytes 3145732
  212.6 4.7 %copy-start.5 = (bf16[1,64,8192]{2,1,0:T(8,128)(2,1)S(1)}, bf16[1,64,8192]{2,1,0:T(8,128)(2,1)}, u32[]{:S(2)}) copy-start(bf16[1,64,8192]{2,1,0:T(8,128)(2,1)} %param.12) | copy-start | bytes 3145732
  212.6 4.7 %copy-start.8 = (bf16[1,64,8192]{2,1,0:T(8,128)(2,1)S(1)}, bf16[1,64,8192]{2,1,0:T(8,128)(2,1)}, u32[]{:S(2)}) copy-start(bf16[1,64,8192]{2,1,0:T(8,128)(2,1)} %param.10) | copy-start | bytes 3145732
  212.6 4.7 %copy-start.10 = (f32[8192,32]{0,1:T(8,128)S(1)}, f32[8192,32]{0,1:T(8,128)}, u32[]{:S(2)}) copy-start(f32[8192,32]{0,1:T(8,128)} %get-tuple-element.7) | copy-start | bytes 3145732
Sparse Core Ops, SparseCore 0:
  82.4 130.1 all-reduce.4
where the time goes:
time: 229 us; the launch traced here: 227 us
  waiting for transfers between devices  130 us (57%)
  blocking collectives  49 us (21%)
  matrix products  19.2 us (8%)
  between operations  14.2 us (6%)
  other arithmetic  13.4 us (6%)
    psum x1, waiting for transfers between devices, per_device(): lax.psum((inner(gate_full, gate_basis), inner(up_full, up_basis)), ('dp',...  130 us
    psum x1, blocking collectives, per_device(): gate_left, up_left = lax.psum((gate_term, up_term), 'dp')  31.1 us
    psum x1, blocking collectives, per_device(): lax.psum((inner(gate_left, gate_left), inner(up_left, up_left)), 'tensor')  17.9 us
    another operation x6, other arithmetic, orthonormal(): lower = jnp.linalg.cholesky(gram)  7.18 us
    another operation x4, other arithmetic, orthonormal(): lax.linalg.triangular_solve(lower, left, left_side=False, lower=True, tra...  6.17 us
    dot_general x4, matrix products, inner(): return jnp.dot(first.T, second, precision=lax.Precision.HIGHEST)  5.26 us
    dot_general x1, matrix products, per_device(): jnp.dot(gate_basis, gate_right.T, precision=lax.Precision.HIGHEST)  4.68 us
  transfers between devices with their start and end apart: 1, of which 1 were waited for; matrix products, arithmetic and copies ran while one was open for 0% of the time, Pallas kernels for 0%

commit v1 on v0

v1 whole, which is shorter than its diff:
```python
import functools

import jax
import jax.numpy as jnp
from jax import lax
from jax.experimental import pallas as pl
from jax.experimental.pallas import tpu as pltpu
from jax.sharding import PartitionSpec as P

F32 = jnp.float32
BF16 = jnp.bfloat16
HIGHEST = lax.Precision.HIGHEST
LOADS = 4
CHUNKS = 2
BLOCK = 512


def split3(x):
    a = x.astype(BF16)
    r = x - a.astype(F32)
    b = r.astype(BF16)
    c = (r - b.astype(F32)).astype(BF16)
    return a, b, c


def spd_inverse(a):
    n = a.shape[0]
    rows = lax.broadcasted_iota(jnp.int32, (n, n), 0)
    cols = lax.broadcasted_iota(jnp.int32, (n, n), 1)
    for k in range(n):
        row = a[k:k + 1, :]
        col = a[:, k:k + 1]
        inv = 1.0 / row[:, k:k + 1]
        scaled = row * inv
        new = jnp.where(cols == k, -col * inv, a - col * scaled)
        a = jnp.where(rows == k, jnp.where(cols == k, inv, scaled), new)
    return a


class Plan:
    def __init__(self, ndp, nt, cols, rank):
        self.core = ("tensor", 1, 2)
        self.y = ("tensor", 2, nt // 2)
        self.x = ("dp", 1, 2)
        self.z = ("dp", 2, ndp // 2)
        self.orders = ((self.core, self.x, self.y, self.z), (self.core, self.y, self.x, self.z))
        self.tiles = (rank // 8) * (cols // 128)
        self.half = self.tiles // 2
        shards = (ndp * nt) // 2
        self.chunks = max(1, min(CHUNKS, self.half // shards))
        assert self.half % (shards * self.chunks) == 0
        self.sizes = []
        for order in self.orders:
            t = [self.half // self.chunks]
            for _, _, n in order[1:]:
                t.append(t[-1] // n)
            self.sizes.append(t)
        self.stages = 4
        self.copies = sum(n - 1 for _, _, n in self.orders[0])


def kernel(plan, ndp, nt, rank, *refs):
    grads, errors, starts = refs[0:2], refs[2:4], refs[4:6]
    w_out, c_out = refs[6:8]
    (ge, st, pbuf, gbuf, part, full, cbuf) = refs[8:15]
    k = 15
    recv = (refs[k:k + 4], refs[k + 4:k + 8])
    acc = (refs[k + 8:k + 11], refs[k + 11:k + 14])
    k += 14
    (load_sem, p_send, p_recv, g_send, g_recv, rs_send, rs_recv, ag_send, ag_recv, out_sem) = refs[k:]

    idx = {"dp": lax.axis_index("dp"), "tensor": lax.axis_index("tensor")}
    size = {"dp": ndp, "tensor": nt}

    def device(axis, i):
        return (i, idx["tensor"]) if axis == "dp" else (idx["dp"], i)

    barrier = pltpu.get_barrier_semaphore()
    for axis in ("dp", "tensor"):
        for o in range(1, size[axis]):
            pl.semaphore_signal(barrier, inc=1, device_id=device(axis, lax.rem(idx[axis] + o, size[axis])),
                                device_id_type=pl.DeviceIdType.MESH)

    n_local, cols = grads[0].shape
    width = cols // LOADS
    loads = {}
    for p in range(2):
        for b in range(LOADS):
            span = pl.ds(b * width, width)
            trio = (
                (starts[p].at[:, span], st.at[p, :, span]),
                (grads[p].at[:, span], ge.at[p, pl.ds(0, n_local), span]),
                (errors[p].at[:, span], ge.at[p, pl.ds(n_local, n_local), span]),
            )
            for m, (src, dst) in enumerate(trio):
                copy = pltpu.make_async_copy(src, dst, load_sem.at[p, b, m])
                copy.start()
                loads[p, b, m] = copy

    terms = []
    for p in range(2):
        total = jnp.zeros((3 * rank, 2 * n_local), F32)
        for b in range(LOADS):
            for m in range(3):
                loads[p, b, m].wait()
            s3 = jnp.concatenate(split3(st[p, :, b * width:(b + 1) * width]), axis=0)
            total += lax.dot_general(s3, ge[p, :, b * width:(b + 1) * width], (((1,), (1,)), ((), ())),
                                     preferred_element_type=F32)
        t = (total[2 * rank:] + total[rank:2 * rank]) + total[:rank]
        terms.append(t[:, :n_local] + t[:, n_local:])
    pbuf[0] = jnp.concatenate(terms, axis=1)

    pl.semaphore_wait(barrier, ndp + nt - 2)
    sends = []

    def exchange(buf, axis, send_sem, recv_sem):
        n = size[axis]
        copies = []
        for o in range(1, n):
            copy = pltpu.make_async_remote_copy(
                src_ref=buf.at[0], dst_ref=buf.at[o], send_sem=send_sem.at[o - 1], recv_sem=recv_sem.at[o - 1],
                device_id=device(axis, lax.rem(idx[axis] + o, n)), device_id_type=pl.DeviceIdType.MESH)
            copy.start()
            copies.append(copy)
        sends.extend(copies)
        return copies

    def summed(buf, axis):
        n = size[axis]
        out = None
        for source in range(n):
            term = buf[lax.rem(idx[axis] - source + n, n)]
            out = term if out is None else out + term
        return out

    copies = exchange(pbuf, "dp", p_send, p_recv)
    for copy in copies:
        copy.wait_recv()
    left = summed(pbuf, "dp") * (1.0 / ndp)
    lefts = [left[:, :n_local], left[:, n_local:]]

    grams = [lax.dot_general(x, x, (((1,), (1,)), ((), ())), precision=HIGHEST, preferred_element_type=F32)
             for x in lefts]
    for p in range(2):
        gbuf[0, p] = grams[p]
    gram_copies = exchange(gbuf, "tensor", g_send, g_recv)

    pieces = [jnp.concatenate(split3(jnp.concatenate([x, x], axis=1)), axis=0) for x in lefts]

    coords = {}
    for order in plan.orders:
        for axis, stride, n in order:
            coords[axis, stride, n] = lax.rem(idx[axis] // stride, n)

    def peer(stage, coordinate):
        axis, stride, n = stage
        return device(axis, idx[axis] + (coordinate - coords[stage]) * stride)

    def right_term(p, j, h):
        first = h * plan.half + j * plan.sizes[p][0]
        columns = plan.sizes[p][0] * 8 * 128 // rank
        block = min(BLOCK, columns)
        per = rank // 8

        def body(i, _):
            tile = first + i * (block // 128 * per)
            col = pl.multiple_of(tile // per * 128, 128)
            w = jnp.dot(pieces[p], ge[p, :, pl.ds(col, block)], preferred_element_type=F32)
            w = (w[2 * rank:] + w[rank:2 * rank]) + w[:rank]
            for b in range(block // 128):
                part[p, pl.ds(tile + b * per, per)] = w[:, b * 128:(b + 1) * 128].reshape(per, 8, 128)
            return 0

        lax.fori_loop(0, columns // block, body, 0, unroll=True)

    def current(p, s, j, d):
        t = plan.sizes[p][s]
        if s == 0:
            return part.at[p, pl.ds(d * plan.half + j * t, t)]
        return acc[p][s - 1].at[j, pl.ds(d * t, t)]

    def offset(p, s, j, last=None):
        out = coords[plan.core] * plan.half if s or last is None else last * plan.half
        out += j * plan.sizes[p][0]
        for i in range(1, s + 1):
            stage = plan.orders[p][i]
            out += (last if i == s and last is not None else coords[stage]) * plan.sizes[p][i]
        return out

    first_sem = [[sum(n - 1 for _, _, n in plan.orders[p][:s]) for s in range(4)] for p in range(2)]
    waiting = {}

    def scatter_start(p, s, j):
        stage = plan.orders[p][s]
        n = stage[2]
        for o in range(1, n):
            to = lax.rem(coords[stage] + o, n)
            q = first_sem[p][s] + o - 1
            copy = pltpu.make_async_remote_copy(
                src_ref=current(p, s, j, to), dst_ref=recv[p][s].at[j, o - 1],
                send_sem=rs_send.at[p, j, q], recv_sem=rs_recv.at[p, j, q],
                device_id=peer(stage, to), device_id_type=pl.DeviceIdType.MESH)
            copy.start()
            sends.append(copy)
            waiting.setdefault((0, p, s, j), []).append(copy)

    def scatter_finish(p, s, j):
        stage = plan.orders[p][s]
        for copy in waiting[0, p, s, j]:
            copy.wait_recv()
        total = current(p, s, j, coords[stage])[...]
        for o in range(1, stage[2]):
            total = total + recv[p][s][j, o - 1]
        if s < 3:
            acc[p][s][j] = total
        else:
            full[p, pl.ds(offset(p, 3, j), plan.sizes[p][3])] = total

    def gather_start(p, s, j):
        stage = plan.orders[p][s]
        n = stage[2]
        t = plan.sizes[p][s]
        mine = full.at[p, pl.ds(offset(p, s, j), t)]
        for o in range(1, n):
            to = lax.rem(coords[stage] + o, n)
            source = lax.rem(coords[stage] - o + n, n)
            q = first_sem[p][s] + o - 1
            common = dict(send_sem=ag_send.at[p, j, q], recv_sem=ag_recv.at[p, j, q],
                          device_id=peer(stage, to), device_id_type=pl.DeviceIdType.MESH)
            copy = pltpu.make_async_remote_copy(src_ref=mine, dst_ref=mine, **common)
            copy.start()
            sends.append(copy)
            arrival = pltpu.make_async_remote_copy(
                src_ref=mine, dst_ref=full.at[p, pl.ds(offset(p, s, j, source), t)], **common)
            waiting.setdefault((1, p, s, j), []).append(arrival)

    def gather_finish(p, s, j):
        for copy in waiting[1, p, s, j]:
            copy.wait_recv()

    outs = []

    def step(p, j, s):
        core = coords[plan.core]
        if s == 0:
            right_term(p, j, 1 - core)
            scatter_start(p, 0, j)
            right_term(p, j, core)
        elif s <= 4:
            scatter_finish(p, s - 1, j)
            if s < 4:
                scatter_start(p, s, j)
            else:
                gather_start(p, 3, j)
        elif s <= 8:
            gather_finish(p, 8 - s, j)
            if s < 8:
                gather_start(p, 7 - s, j)
            else:
                t = plan.sizes[p][0]
                for h in range(2):
                    span = pl.ds(h * plan.half + j * t, t)
                    copy = pltpu.make_async_copy(full.at[p, span], w_out.at[p, span], out_sem.at[p, j, h])
                    copy.start()
                    outs.append(copy)

    def coefficients():
        for copy in gram_copies:
            copy.wait_recv()
        for p in range(2):
            gram = None
            for source in range(nt):
                term = gbuf[lax.rem(idx["tensor"] - source + nt, nt), p]
                gram = term if gram is None else gram + term
            c = jnp.dot(spd_inverse(gram), lefts[p], precision=HIGHEST, preferred_element_type=F32) * (1.0 / ndp)
            c0, c1, c2 = split3(c)
            cbuf[p] = jnp.concatenate([c0, c0, c0, c1, c1, c2], axis=0)
        copy = pltpu.make_async_copy(cbuf, c_out, out_sem.at[0, 0, 2])
        copy.start()
        outs.append(copy)

    for wave in range(9 + plan.chunks - 1):
        for j in range(plan.chunks):
            for p in range(2):
                if 0 <= wave - j <= 8:
                    step(p, j, wave - j)
        if wave == 2:
            coefficients()

    for copy in sends:
        copy.wait_send()
    for copy in outs:
        copy.wait()


def finish_kernel(rank, w_ref, c_ref, g0, g1, e0, e1, m0, m1, n0, n1):
    per = rank // 8
    width = g0.shape[1]
    for p, (g, e, m, new) in enumerate(((g0, e0, m0, n0), (g1, e1, m1, n1))):
        w = jnp.concatenate(
            [w_ref[p, b * per:(b + 1) * per].reshape(rank, 128) for b in range(width // 128)], axis=1)
        w0, w1, w2 = split3(w)
        w6 = jnp.concatenate([w0, w1, w2, w0, w1, w0], axis=0)
        a = lax.dot_general(c_ref[p], w6, (((0,), (0,)), ((), ())), preferred_element_type=F32)
        m[...] = a.astype(BF16)
        new[...] = (g[...].astype(F32) + e[...].astype(F32) - a).astype(BF16)


def per_device(ndp, nt, gate_grads, up_grads, gate_errors, up_errors, gate_start, up_start):
    grads = (gate_grads[0], up_grads[0])
    errors = (gate_errors[0], up_errors[0])
    starts = (gate_start.T, up_start.T)
    n_local, cols = grads[0].shape
    rank = gate_start.shape[1]
    plan = Plan(ndp, nt, cols, rank)
    dma = pltpu.SemaphoreType.DMA
    tile = (8, 128)
    j = plan.chunks
    scratch = [
        pltpu.VMEM((2, 2 * n_local, cols), BF16),
        pltpu.VMEM((2, rank, cols), F32),
        pltpu.VMEM((ndp, rank, 2 * n_local), F32),
        pltpu.VMEM((nt, 2, rank, rank), F32),
        pltpu.VMEM((2, plan.tiles) + tile, F32),
        pltpu.VMEM((2, plan.tiles) + tile, F32),
        pltpu.VMEM((2, 6 * rank, n_local), BF16),
    ]
    for p in range(2):
        for s in range(4):
            scratch.append(pltpu.VMEM((j, plan.orders[p][s][2] - 1, plan.sizes[p][s]) + tile, F32))
    for p in range(2):
        for s in range(3):
            scratch.append(pltpu.VMEM((j, plan.sizes[p][s]) + tile, F32))
    scratch += [
        dma((2, LOADS, 3)),
        dma((ndp - 1,)), dma((ndp - 1,)), dma((nt - 1,)), dma((nt - 1,)),
        dma((2, j, plan.copies)), dma((2, j, plan.copies)), dma((2, j, plan.copies)), dma((2, j, plan.copies)),
        dma((2, j, 3)),
    ]
    anywhere = pl.BlockSpec(memory_space=pl.ANY)
    w, c = pl.pallas_call(
        functools.partial(kernel, plan, ndp, nt, rank),
        out_shape=(jax.ShapeDtypeStruct((2, plan.tiles) + tile, F32),
                   jax.ShapeDtypeStruct((2, 6 * rank, n_local), BF16)),
        in_specs=[anywhere] * 6,
        out_specs=(anywhere, anywhere),
        scratch_shapes=scratch,
        compiler_params=pltpu.CompilerParams(collective_id=0, has_side_effects=True,
                                             vmem_limit_bytes=32 * 1024 * 1024),
        name="reduce_right",
    )(*grads, *errors, *starts)

    blocks = 4
    width = cols // blocks
    wide = pl.BlockSpec((n_local, width), lambda i: (0, i))
    gate_mean, up_mean, gate_new, up_new = pl.pallas_call(
        functools.partial(finish_kernel, rank),
        grid=(blocks,),
        out_shape=(jax.ShapeDtypeStruct((n_local, cols), BF16),) * 4,
        in_specs=[pl.BlockSpec((2, plan.tiles // blocks) + tile, lambda i: (0, i, 0, 0)),
                  pl.BlockSpec((2, 6 * rank, n_local), lambda i: (0, 0, 0))] + [wide] * 4,
        out_specs=(wide,) * 4,
        compiler_params=pltpu.CompilerParams(vmem_limit_bytes=32 * 1024 * 1024),
        name="form_outputs",
    )(w, c, *grads, *errors)
    return gate_mean, up_mean, gate_new[None], up_new[None]


def solution(mesh):
    rows = P("dp", "tensor", None)
    return jax.shard_map(
        functools.partial(per_device, mesh.shape["dp"], mesh.shape["tensor"]),
        mesh=mesh,
        in_specs=(rows, rows, rows, rows, P(), P()),
        out_specs=(P("tensor", None), P("tensor", None), rows, rows),
        check_vma=False,
    )
```

time: 229 us -> 64.1 us (0.28)
  waiting for transfers between devices: 130 us -> 0 us
  Pallas kernels: 0 us -> 55.7 us
  blocking collectives: 49 us -> 0 us
  matrix products: 19.2 us -> 0 us
  between operations: 14.2 us -> 0.65 us
  other arithmetic: 13.4 us -> 0 us
  local copies, waits for them, and re-layouts: 1.37 us -> 7.34 us
    psum x1 -> x0, waiting for transfers between devices: 130 us -> none  [per_device(): lax.psum((inner(gate_full, gate_basis), inner(up_full, up_basis)), ('dp',...]
    pallas_call x0 -> x2, Pallas kernels: none -> 55.7 us  [the longest x1 52.2 us: per_device(): pl.pallas_call(functools.partial(kernel, plan, ndp, nt, rank), out_shape=...]
    psum x2 -> x0, blocking collectives: 49 us -> none  [the longest x1 31.1 us: per_device(): gate_left, up_left = lax.psum((gate_term, up_term), 'dp')]
    dot_general x8 -> x0, matrix products: 18.8 us -> none  [the longest x4 5.26 us: inner(): return jnp.dot(first.T, second, precision=lax.Precision.HIGHEST)]
    another operation x10 -> x0, other arithmetic: 13.4 us -> none  [the longest x6 7.18 us: orthonormal(): lower = jnp.linalg.cholesky(gram)]
    unnamed x22 -> x12, local copies, waits for them, and re-layouts: 1.22 us -> 7.34 us
  transfers between devices with their start and end apart: 1 -> 0, of which waited for: 1 -> 0; matrix products, arithmetic and copies ran while one was open for 0% -> 0% of each run, Pallas kernels for 0% -> 0%
where the time goes in v1:
time: 64.1 us; the launch traced here: 63.7 us
  Pallas kernels  55.7 us (87%)
  local copies, waits for them, and re-layouts  7.34 us (11%)
  between operations  0.65 us (1%)
    pallas_call x1, Pallas kernels, per_device(): pl.pallas_call(functools.partial(kernel, plan, ndp, nt, rank), out_shape=...  52.2 us
    unnamed x12, local copies, waits for them, and re-layouts  7.34 us
    pallas_call x1, Pallas kernels, per_device(): pl.pallas_call(functools.partial(finish_kernel, rank), grid=(blocks,), ou...  3.53 us

profile of v1, /device:TPU:1, one launch (start us, length us, event | category | flops | bytes accessed | tf_op | source)
XLA Modules:
  0.0 63.7 jit_solution(18023890778330288578)
XLA Ops:
  0.6 0.0 copy-start
  0.6 1.2 %copy-done = bf16[1,64,8192]{2,1,0:T(8,128)(2,1)S(1)} copy-done((bf16[1,64,8192]{2,1,0:T(8,128)(2,1)S(1)}, bf16[1,64,8192]{2,1,0:T(8,128)(2,1)}, u32[]{:S(2)}) %copy-start) | copy-done | bytes 1048600
  1.9 0.0 copy-start.1
  1.9 1.2 %copy-done.1 = bf16[1,64,8192]{2,1,0:T(8,128)(2,1)S(1)} copy-done((bf16[1,64,8192]{2,1,0:T(8,128)(2,1)S(1)}, bf16[1,64,8192]{2,1,0:T(8,128)(2,1)}, u32[]{:S(2)}) %copy-start.1) | copy-done | bytes 1048600
  3.1 0.0 copy-start.2
  3.1 1.2 %copy-done.2 = bf16[1,64,8192]{2,1,0:T(8,128)(2,1)S(1)} copy-done((bf16[1,64,8192]{2,1,0:T(8,128)(2,1)S(1)}, bf16[1,64,8192]{2,1,0:T(8,128)(2,1)}, u32[]{:S(2)}) %copy-start.2) | copy-done | bytes 1048600
  4.3 0.0 copy-start.3
  4.3 1.2 %copy-done.3 = bf16[1,64,8192]{2,1,0:T(8,128)(2,1)S(1)} copy-done((bf16[1,64,8192]{2,1,0:T(8,128)(2,1)S(1)}, bf16[1,64,8192]{2,1,0:T(8,128)(2,1)}, u32[]{:S(2)}) %copy-start.3) | copy-done | bytes 1048600
  5.5 0.0 copy-start.4
  5.5 1.2 %copy-done.4 = f32[8192,32]{0,1:T(8,128)S(1)} copy-done((f32[8192,32]{0,1:T(8,128)S(1)}, f32[8192,32]{0,1:T(8,128)}, u32[]{:S(2)}) %copy-start.4) | copy-done | bytes 1048600
  6.8 0.0 copy-start.5
  6.8 1.2 %copy-done.5 = f32[8192,32]{0,1:T(8,128)S(1)} copy-done((f32[8192,32]{0,1:T(8,128)S(1)}, f32[8192,32]{0,1:T(8,128)}, u32[]{:S(2)}) %copy-start.5) | copy-done | bytes 1048600
  8.0 52.2 %reduce_right.1 = (f32[2,256,8,128]{3,2,1,0:T(8,128)S(1)}, bf16[2,192,64]{2,1,0:T(8,128)(2,1)S(1)}) custom-call(bf16[64,8192]{1,0:T(8,128)(2,1)S(1)} %bitcast.8, bf16[64,8192]{1,0:T(8,128)(2,1)S(1)} %bitcast.10, bf16[64,8192]{1,0:T(8,128)(2,1)S(1)} %bitcast.12, bf16[64,8192]{1,0:T(8,128)(2,1)S(1)} %bitcast.14, f32[32,8192]{1,0:T(8,128)S(1)} %bitcast.16, ...), custom_call_target="tpu_custom_call" | custom-call | tf_op jit(solution)/shard_map/reduce_right/pallas_call | solution.py:341
  60.2 3.5 %form_outputs.1 = (bf16[64,8192]{1,0:T(8,128)(2,1)}, bf16[64,8192]{1,0:T(8,128)(2,1)}, bf16[64,8192]{1,0:T(8,128)(2,1)}, bf16[64,8192]{1,0:T(8,128)(2,1)}) custom-call(f32[2,256,8,128]{3,2,1,0:T(8,128)S(1)} %get-tuple-element.10.w_ref, bf16[2,192,64]{2,1,0:T(8,128)(2,1)S(1)} %get-tuple-element.11.c_ref, bf16[64,8192]{1,0:T(8,128)(2,1)S(1)} %bitcast.9, ...), custom_call_target="tpu_custom_call" | custom-call | tf_op jit(solution)/shard_map/form_outputs/pallas_call | solution.py:356
Async XLA Ops:
  0.6 1.2 %copy-start = (bf16[1,64,8192]{2,1,0:T(8,128)(2,1)S(1)}, bf16[1,64,8192]{2,1,0:T(8,128)(2,1)}, u32[]{:S(2)}) copy-start(bf16[1,64,8192]{2,1,0:T(8,128)(2,1)} %param.6) | copy-start | bytes 3145732
  1.9 1.2 %copy-start.1 = (bf16[1,64,8192]{2,1,0:T(8,128)(2,1)S(1)}, bf16[1,64,8192]{2,1,0:T(8,128)(2,1)}, u32[]{:S(2)}) copy-start(bf16[1,64,8192]{2,1,0:T(8,128)(2,1)} %param.7) | copy-start | bytes 3145732
  3.1 1.2 %copy-start.2 = (bf16[1,64,8192]{2,1,0:T(8,128)(2,1)S(1)}, bf16[1,64,8192]{2,1,0:T(8,128)(2,1)}, u32[]{:S(2)}) copy-start(bf16[1,64,8192]{2,1,0:T(8,128)(2,1)} %param.8) | copy-start | bytes 3145732
  4.3 1.2 %copy-start.3 = (bf16[1,64,8192]{2,1,0:T(8,128)(2,1)S(1)}, bf16[1,64,8192]{2,1,0:T(8,128)(2,1)}, u32[]{:S(2)}) copy-start(bf16[1,64,8192]{2,1,0:T(8,128)(2,1)} %param.9) | copy-start | bytes 3145732
  5.5 1.2 %copy-start.4 = (f32[8192,32]{0,1:T(8,128)S(1)}, f32[8192,32]{0,1:T(8,128)}, u32[]{:S(2)}) copy-start(f32[8192,32]{0,1:T(8,128)} %param.10) | copy-start | bytes 3145732
  6.8 1.2 %copy-start.5 = (f32[8192,32]{0,1:T(8,128)S(1)}, f32[8192,32]{0,1:T(8,128)}, u32[]{:S(2)}) copy-start(f32[8192,32]{0,1:T(8,128)} %param.11) | copy-start | bytes 3145732

commit v2 on v1

--- a/solution.py
+++ b/solution.py
@@ -23,11 +23,11 @@
     return a, b, c
 
 
-def spd_inverse(a):
+def inverse_steps(a, steps):
     n = a.shape[0]
     rows = lax.broadcasted_iota(jnp.int32, (n, n), 0)
     cols = lax.broadcasted_iota(jnp.int32, (n, n), 1)
-    for k in range(n):
+    for k in steps:
         row = a[k:k + 1, :]
         col = a[:, k:k + 1]
         inv = 1.0 / row[:, k:k + 1]
@@ -97,8 +97,7 @@
                 copy.start()
                 loads[p, b, m] = copy
 
-    terms = []
-    for p in range(2):
+    def left_term(p):
         total = jnp.zeros((3 * rank, 2 * n_local), F32)
         for b in range(LOADS):
             for m in range(3):
@@ -107,10 +106,9 @@
             total += lax.dot_general(s3, ge[p, :, b * width:(b + 1) * width], (((1,), (1,)), ((), ())),
                                      preferred_element_type=F32)
         t = (total[2 * rank:] + total[rank:2 * rank]) + total[:rank]
-        terms.append(t[:, :n_local] + t[:, n_local:])
-    pbuf[0] = jnp.concatenate(terms, axis=1)
-
-    pl.semaphore_wait(barrier, ndp + nt - 2)
+        t = t[:, :n_local] + t[:, n_local:]
+        pbuf[p, 0] = jnp.concatenate([t[:rank // 2], t[rank // 2:]], axis=1)
+
     sends = []
 
     def exchange(buf, axis, send_sem, recv_sem):
@@ -133,19 +131,25 @@
             out = term if out is None else out + term
         return out
 
-    copies = exchange(pbuf, "dp", p_send, p_recv)
-    for copy in copies:
-        copy.wait_recv()
-    left = summed(pbuf, "dp") * (1.0 / ndp)
-    lefts = [left[:, :n_local], left[:, n_local:]]
-
-    grams = [lax.dot_general(x, x, (((1,), (1,)), ((), ())), precision=HIGHEST, preferred_element_type=F32)
-             for x in lefts]
-    for p in range(2):
-        gbuf[0, p] = grams[p]
-    gram_copies = exchange(gbuf, "tensor", g_send, g_recv)
-
-    pieces = [jnp.concatenate(split3(jnp.concatenate([x, x], axis=1)), axis=0) for x in lefts]
+    left_term(0)
+    pl.semaphore_wait(barrier, ndp + nt - 2)
+    left_copies = [exchange(pbuf.at[0], "dp", p_send.at[0], p_recv.at[0])]
+    left_term(1)
+    left_copies.append(exchange(pbuf.at[1], "dp", p_send.at[1], p_recv.at[1]))
+    lefts, pieces, gram_copies = {}, {}, {}
+
+    def left_finish(p):
+        for copy in left_copies[p]:
+            copy.wait_recv()
+        x = summed(pbuf.at[p], "dp") * (1.0 / ndp)
+        x = jnp.concatenate([x[:, :n_local], x[:, n_local:]], axis=0)
+        lefts[p] = x
+        pieces[p] = jnp.concatenate(split3(jnp.concatenate([x, x], axis=1)), axis=0)
+
+    def gram_start(p):
+        x = lefts[p]
+        gbuf[p, 0] = lax.dot_general(x, x, (((1,), (1,)), ((), ())), precision=HIGHEST, preferred_element_type=F32)
+        gram_copies[p] = exchange(gbuf.at[p], "tensor", g_send.at[p], g_recv.at[p])
 
     coords = {}
     for order in plan.orders:
@@ -243,8 +247,12 @@
     def step(p, j, s):
         core = coords[plan.core]
         if s == 0:
+            if j == 0:
+                left_finish(p)
             right_term(p, j, 1 - core)
             scatter_start(p, 0, j)
+            if j == 0:
+                gram_start(p)
             right_term(p, j, core)
         elif s <= 4:
             scatter_finish(p, s - 1, j)
@@ -264,27 +272,36 @@
                     copy.start()
                     outs.append(copy)
 
+    inverses = {}
+
+    def inverse_start(p):
+        for copy in gram_copies[p]:
+            copy.wait_recv()
+        inverses[p] = summed(gbuf.at[p], "tensor")
+
     def coefficients():
-        for copy in gram_copies:
-            copy.wait_recv()
         for p in range(2):
-            gram = None
-            for source in range(nt):
-                term = gbuf[lax.rem(idx["tensor"] - source + nt, nt), p]
-                gram = term if gram is None else gram + term
-            c = jnp.dot(spd_inverse(gram), lefts[p], precision=HIGHEST, preferred_element_type=F32) * (1.0 / ndp)
+            c = jnp.dot(inverses[p], lefts[p], precision=HIGHEST, preferred_element_type=F32) * (1.0 / ndp)
             c0, c1, c2 = split3(c)
             cbuf[p] = jnp.concatenate([c0, c0, c0, c1, c1, c2], axis=0)
         copy = pltpu.make_async_copy(cbuf, c_out, out_sem.at[0, 0, 2])
         copy.start()
         outs.append(copy)
 
+    per_wave = -(-rank // 7)
     for wave in range(9 + plan.chunks - 1):
         for j in range(plan.chunks):
             for p in range(2):
                 if 0 <= wave - j <= 8:
                     step(p, j, wave - j)
         if wave == 2:
+            for p in range(2):
+                inverse_start(p)
+        if 2 <= wave <= 8:
+            first = (wave - 2) * per_wave
+            for p in range(2):
+                inverses[p] = inverse_steps(inverses[p], range(first, min(first + per_wave, rank)))
+        if wave == 8:
             coefficients()
 
     for copy in sends:
@@ -319,8 +336,8 @@
     scratch = [
         pltpu.VMEM((2, 2 * n_local, cols), BF16),
         pltpu.VMEM((2, rank, cols), F32),
-        pltpu.VMEM((ndp, rank, 2 * n_local), F32),
-        pltpu.VMEM((nt, 2, rank, rank), F32),
+        pltpu.VMEM((2, ndp, rank // 2, 2 * n_local), F32),
+        pltpu.VMEM((2, nt, rank, rank), F32),
         pltpu.VMEM((2, plan.tiles) + tile, F32),
         pltpu.VMEM((2, plan.tiles) + tile, F32),
         pltpu.VMEM((2, 6 * rank, n_local), BF16),
@@ -333,7 +350,7 @@
             scratch.append(pltpu.VMEM((j, plan.sizes[p][s]) + tile, F32))
     scratch += [
         dma((2, LOADS, 3)),
-        dma((ndp - 1,)), dma((ndp - 1,)), dma((nt - 1,)), dma((nt - 1,)),
+        dma((2, ndp - 1)), dma((2, ndp - 1)), dma((2, nt - 1)), dma((2, nt - 1)),
         dma((2, j, plan.copies)), dma((2, j, plan.copies)), dma((2, j, plan.copies)), dma((2, j, plan.copies)),
         dma((2, j, 3)),
     ]
@@ -346,7 +363,7 @@
         out_specs=(anywhere, anywhere),
         scratch_shapes=scratch,
         compiler_params=pltpu.CompilerParams(collective_id=0, has_side_effects=True,
-                                             vmem_limit_bytes=32 * 1024 * 1024),
+                                             vmem_limit_bytes=62 * 1024 * 1024),
         name="reduce_right",
     )(*grads, *errors, *starts)
 
@@ -360,7 +377,7 @@
         in_specs=[pl.BlockSpec((2, plan.tiles // blocks) + tile, lambda i: (0, i, 0, 0)),
                   pl.BlockSpec((2, 6 * rank, n_local), lambda i: (0, 0, 0))] + [wide] * 4,
         out_specs=(wide,) * 4,
-        compiler_params=pltpu.CompilerParams(vmem_limit_bytes=32 * 1024 * 1024),
+        compiler_params=pltpu.CompilerParams(vmem_limit_bytes=62 * 1024 * 1024),
         name="form_outputs",
     )(w, c, *grads, *errors)
     return gate_mean, up_mean, gate_new[None], up_new[None]

time: 64.1 us -> 55.4 us (0.86)
  local copies, waits for them, and re-layouts: 7.34 us -> 0 us
  Pallas kernels: 55.7 us -> 54.6 us
    unnamed x12 -> x0, local copies, waits for them, and re-layouts: 7.34 us -> none
    pallas_call x1, Pallas kernels: 52.2 us -> 48.8 us  [per_device(): pl.pallas_call(functools.partial(kernel, plan, ndp, nt, rank), out_shape=...]
    pallas_call x1, Pallas kernels: 3.53 us -> 5.74 us  [per_device(): pl.pallas_call(functools.partial(finish_kernel, rank), grid=(blocks,), ou...]
where the time goes in v2:
time: 55.4 us; the launch traced here: 55.2 us
  Pallas kernels  54.6 us (99%)
  between operations  0.64 us (1%)
    pallas_call x1, Pallas kernels, per_device(): pl.pallas_call(functools.partial(kernel, plan, ndp, nt, rank), out_shape=...  48.8 us
    pallas_call x1, Pallas kernels, per_device(): pl.pallas_call(functools.partial(finish_kernel, rank), grid=(blocks,), ou...  5.74 us

profile of v2, /device:TPU:1, one launch (start us, length us, event | category | flops | bytes accessed | tf_op | source)
XLA Modules:
  0.0 55.2 jit_solution(5981862895143600265)
XLA Ops:
  0.6 48.8 %reduce_right.1 = (f32[2,256,8,128]{3,2,1,0:T(8,128)}, bf16[2,192,64]{2,1,0:T(8,128)(2,1)}) custom-call(bf16[64,8192]{1,0:T(8,128)(2,1)} %bitcast.8, bf16[64,8192]{1,0:T(8,128)(2,1)} %bitcast.10, bf16[64,8192]{1,0:T(8,128)(2,1)} %bitcast.12, bf16[64,8192]{1,0:T(8,128)(2,1)} %bitcast.14, f32[32,8192]{1,0:T(8,128)} %bitcast.16, f32[32,8192]{1,0:T(8,128)} %bitcast.17), custom_call_target="tpu_custom_call" | custom-call | tf_op jit(solution)/shard_map/reduce_right/pallas_call | solution.py:358
  49.5 5.7 %form_outputs.1 = (bf16[64,8192]{1,0:T(8,128)(2,1)}, bf16[64,8192]{1,0:T(8,128)(2,1)}, bf16[64,8192]{1,0:T(8,128)(2,1)}, bf16[64,8192]{1,0:T(8,128)(2,1)}) custom-call(f32[2,256,8,128]{3,2,1,0:T(8,128)} %get-tuple-element.10.w_ref, bf16[2,192,64]{2,1,0:T(8,128)(2,1)} %get-tuple-element.11.c_ref, bf16[64,8192]{1,0:T(8,128)(2,1)} %bitcast.9, ...), custom_call_target="tpu_custom_call" | custom-call | tf_op jit(solution)/shard_map/form_outputs/pallas_call | solution.py:373

commit v3 on v2

--- a/solution.py
+++ b/solution.py
@@ -367,7 +367,7 @@
         name="reduce_right",
     )(*grads, *errors, *starts)
 
-    blocks = 4
+    blocks = 2
     width = cols // blocks
     wide = pl.BlockSpec((n_local, width), lambda i: (0, i))
     gate_mean, up_mean, gate_new, up_new = pl.pallas_call(

time: 55.4 us -> 54.4 us (0.982)
  Pallas kernels: 54.6 us -> 53.6 us
    pallas_call x1, Pallas kernels: 5.74 us -> 4.76 us  [per_device(): pl.pallas_call(functools.partial(finish_kernel, rank), grid=(blocks,), ou...]
where the time goes in v3:
time: 54.4 us; the launch traced here: 54.2 us
  Pallas kernels  53.6 us (99%)
  between operations  0.64 us (1%)
    pallas_call x1, Pallas kernels, per_device(): pl.pallas_call(functools.partial(kernel, plan, ndp, nt, rank), out_shape=...  48.8 us
    pallas_call x1, Pallas kernels, per_device(): pl.pallas_call(functools.partial(finish_kernel, rank), grid=(blocks,), ou...  4.76 us

profile of v3, /device:TPU:1, one launch (start us, length us, event | category | flops | bytes accessed | tf_op | source)
XLA Modules:
  0.0 54.2 jit_solution(8017506330995023725)
XLA Ops:
  0.6 48.8 %reduce_right.1 = (f32[2,256,8,128]{3,2,1,0:T(8,128)}, bf16[2,192,64]{2,1,0:T(8,128)(2,1)}) custom-call(bf16[64,8192]{1,0:T(8,128)(2,1)} %bitcast.8, bf16[64,8192]{1,0:T(8,128)(2,1)} %bitcast.10, bf16[64,8192]{1,0:T(8,128)(2,1)} %bitcast.12, bf16[64,8192]{1,0:T(8,128)(2,1)} %bitcast.14, f32[32,8192]{1,0:T(8,128)} %bitcast.16, f32[32,8192]{1,0:T(8,128)} %bitcast.17), custom_call_target="tpu_custom_call" | custom-call | tf_op jit(solution)/shard_map/reduce_right/pallas_call | solution.py:358
  49.5 4.8 %form_outputs.1 = (bf16[64,8192]{1,0:T(8,128)(2,1)}, bf16[64,8192]{1,0:T(8,128)(2,1)}, bf16[64,8192]{1,0:T(8,128)(2,1)}, bf16[64,8192]{1,0:T(8,128)(2,1)}) custom-call(f32[2,256,8,128]{3,2,1,0:T(8,128)} %get-tuple-element.10.w_ref, bf16[2,192,64]{2,1,0:T(8,128)(2,1)} %get-tuple-element.11.c_ref, bf16[64,8192]{1,0:T(8,128)(2,1)} %bitcast.9, ...), custom_call_target="tpu_custom_call" | custom-call | tf_op jit(solution)/shard_map/form_outputs/pallas_call | solution.py:373
